TPU v7x, 512 devices: a whole 4x8x8 slice. The times are simulated.
512 devices in a mesh: patch: 128 (over z, x_hi, y), head: 4 (over x_lo, core).
Axes of the slice: x: 4 (x_hi: 2, x_lo: 2; x = x_hi * 2 + x_lo), y: 8, z: 8, core: 2. Of those that a mesh axis runs over, the one named last changes fastest.
Arguments:
- queries: bfloat16 [32768, 3072], P(('patch', 'head')), may hold values from -16 to 16
- keys: bfloat16 [32768, 3072], P(('patch', 'head')), may hold values from -5 to 5
- values: bfloat16 [32768, 3072], P(('patch', 'head')), may hold values from -6 to 6
Outputs:
- attended: bfloat16 [32768, 3072], P(('patch', 'head'))
All inputs are finite; a program needn't handle non-finite values.
Results may differ from a plain program's by a relative error of at most 0.0085.
Values may be sent and summed in bfloat16 or wider, within the bound.
A program may use at most 128 MiB of HBM per device.

v0:
```python
import jax
import jax.numpy as jnp
from jax import lax
from jax.sharding import PartitionSpec as P

HD = 128
POOL = 16


def pool_tokens(array):
    grouped = array.reshape(array.shape[0] // POOL, POOL, array.shape[1]).astype(jnp.float32)
    return jnp.mean(grouped, axis=1).astype(jnp.bfloat16)


def block_length(total_rows):
    for length in range(min(total_rows, 512), 0, -1):
        if total_rows % length == 0:
            return length
    return 1


def fold_blocks(carry, key_piece, value_piece, query_heads):
    total_rows = key_piece.shape[0]
    heads_here = query_heads.shape[1]
    length = block_length(total_rows)
    score_scale = HD ** (-0.5)
    key_blocks = key_piece.reshape(total_rows // length, length, heads_here, HD)
    value_blocks = value_piece.reshape(total_rows // length, length, heads_here, HD)

    def update(state, block_pair):
        maxima, totals, accum = state
        key_block, value_block = block_pair
        scores = (
            jnp.einsum("qhd,khd->hqk", query_heads, key_block, preferred_element_type=jnp.float32)
            * score_scale
        )
        newest = jnp.maximum(maxima, jnp.max(scores, axis=2))
        rescale = jnp.exp(maxima - newest)
        exponent = jnp.exp(scores - newest[:, :, None])
        totals = totals * rescale + jnp.sum(exponent, axis=2)
        weights = exponent.astype(jnp.bfloat16)
        accum = accum * rescale[:, :, None] + jnp.einsum(
            "hqk,khd->hqd", weights, value_block, preferred_element_type=jnp.float32
        )
        return ((newest, totals, accum), None)

    result, unused = lax.scan(update, carry, (key_blocks, value_blocks))
    return result


def shards(queries, keys, values):
    tok_dev, width = queries.shape
    groups = lax.axis_size("head")
    columns = width // groups
    heads_here = columns // HD
    query_rows = tok_dev * groups
    local_queries, local_keys, local_values = (
        lax.all_to_all(queries, "head", split_axis=1, concat_axis=0, tiled=True),
        lax.all_to_all(keys, "head", split_axis=1, concat_axis=0, tiled=True),
        lax.all_to_all(values, "head", split_axis=1, concat_axis=0, tiled=True),
    )
    key_rows = pool_tokens(local_keys)
    value_rows = pool_tokens(local_values)
    query_heads = local_queries.reshape(query_rows, heads_here, HD)
    start_state = (
        jnp.full((heads_here, query_rows), -1e30, jnp.float32),
        jnp.zeros((heads_here, query_rows), jnp.float32),
        jnp.zeros((heads_here, query_rows, HD), jnp.float32),
    )
    final_state = fold_blocks(
        start_state,
        lax.all_gather(key_rows, "patch", axis=0, tiled=True),
        lax.all_gather(value_rows, "patch", axis=0, tiled=True),
        query_heads,
    )
    maxima, totals, accum = final_state
    mixed = accum / totals[:, :, None]
    power = jnp.mean(mixed * mixed, axis=2, keepdims=True)
    normed = (mixed / jnp.sqrt(power + 1e-06)).astype(jnp.bfloat16)
    outgoing = normed.transpose(1, 0, 2).reshape(query_rows, columns)
    return lax.all_to_all(outgoing, "head", split_axis=0, concat_axis=1, tiled=True)


def solution(mesh):
    return jax.shard_map(
        shards,
        mesh=mesh,
        in_specs=(
            P(("patch", "head"), None),
            P(("patch", "head"), None),
            P(("patch", "head"), None),
        ),
        out_specs=P(("patch", "head"), None),
        check_vma=False,
    )
```

profile of v0, /device:TPU:1, one launch (start us, length us, event | category | flops | bytes accessed | tf_op | source)
XLA Modules:
  0.0 347.9 jit_solution(10728279585370942899)
XLA Ops:
  6.5 1.1 copy.45
  7.6 15.8 %all_to_all.61 = bf16[64,4,768]{2,0,1:T(8,128)(2,1)S(1)} all-to-all(bf16[64,4,768]{2,0,1:T(8,128)(2,1)S(1)} %bitcast.61), channel_id=1, replica_groups=mesh['patch'=128,'head'=4] {'head'}, dimensions={1} | all-to-all | bytes 786432 | tf_op jit(solution)/shard_map/all_to_all | solution.py:59
  23.6 0.6 multiply_convert_fusion.1
  24.4 9.8 %all_to_all.62 = bf16[64,4,768]{2,0,1:T(8,128)(2,1)S(1)} all-to-all(bf16[64,4,768]{2,0,1:T(8,128)(2,1)S(1)} %bitcast.62), channel_id=1, replica_groups=mesh['patch'=128,'head'=4] {'head'}, dimensions={1} | all-to-all | bytes 786432 | tf_op jit(solution)/shard_map/all_to_all | solution.py:60
  34.4 0.6 multiply_convert_fusion
  35.0 0.8 copy.44
  35.8 4.5 %all-to-all-start.1 = ((bf16[64,4,768]{2,0,1:T(8,128)(2,1)}), bf16[64,4,768]{2,0,1:T(8,128)(2,1)S(1)}, u32[]{:S(2)}, u32[]{:S(2)}) async-start(bf16[64,4,768]{2,0,1:T(8,128)(2,1)} %bitcast.43), calls=%async_computation.1 | async-start | bytes 786432 | tf_op jit(solution)/shard_map/all_to_all | solution.py:58
  40.3 6.7 %all-to-all-done.1 = bf16[64,4,768]{2,0,1:T(8,128)(2,1)S(1)} async-done(((bf16[64,4,768]{2,0,1:T(8,128)(2,1)}), bf16[64,4,768]{2,0,1:T(8,128)(2,1)S(1)}, u32[]{:S(2)}, u32[]{:S(2)}) %all-to-all-start.1) | async-done | bytes 393248 | tf_op jit(solution)/shard_map/all_to_all | solution.py:58
  47.5 106.1 %all-gather.3.cloned.1.call-done = bf16[2048,768]{1,0:T(8,128)(2,1)} async-done(((bf16[16,768]{1,0:T(8,128)(2,1)}), bf16[2048,768]{1,0:T(8,128)(2,1)}) %all-gather.3.cloned.1.call-update) | async-done | bytes 3145744 | tf_op jit(solution)/shard_map/all_gather | solution.py:72
  153.7 7.7 %reshape.48 = bf16[4,512,6,128]{3,2,1,0:T(8,128)(2,1)} reshape(bf16[2048,768]{1,0:T(8,128)(2,1)} %all-gather.3.cloned.1.call-done) | data formatting | bytes 6291456 | tf_op jit(solution)/shard_map/reshape | solution.py:27
  161.3 4.6 %copy.26 = bf16[4,512,6,128]{3,1,2,0:T(8,128)(2,1)} copy(bf16[4,512,6,128]{3,2,1,0:T(8,128)(2,1)} %reshape.48) | data formatting | bytes 6291456
  165.9 120.4 %all-gather.5.cloned.1.call-done = bf16[2048,768]{1,0:T(8,128)(2,1)} async-done(((bf16[16,768]{1,0:T(8,128)(2,1)}), bf16[2048,768]{1,0:T(8,128)(2,1)}) %all-gather.5.cloned.1.call-update) | async-done | bytes 3145744 | tf_op jit(solution)/shard_map/all_gather | solution.py:73
  286.3 7.7 %reshape.49 = bf16[4,512,6,128]{3,2,1,0:T(8,128)(2,1)} reshape(bf16[2048,768]{1,0:T(8,128)(2,1)} %all-gather.5.cloned.1.call-done) | data formatting | bytes 6291456 | tf_op jit(solution)/shard_map/reshape | solution.py:28
  294.0 4.6 %copy.28 = bf16[4,512,6,128]{3,1,2,0:T(8,128)(2,1)} copy(bf16[4,512,6,128]{3,2,1,0:T(8,128)(2,1)} %reshape.49) | data formatting | bytes 6291456
  298.6 24.3 %while.15 = (s32[]{:T(128)}, f32[6,256]{1,0:T(8,128)S(1)}, f32[6,256]{1,0:T(8,128)}, f32[6,256,128]{2,1,0:T(8,128)}, bf16[4,512,6,128]{3,1,2,0:T(8,128)(2,1)}, /...) while((s32[]{:T(128)}, f32[6,256]{1,0:T(8,128)S(1)}, ...), condition=%wide.region_5.6_spmd.clone, body=%wide.region_2.5_spmd.clone.sunk | while | flops 409542144 | bytes 19416280 | solution.py:47
  298.6 1.7 bitcast_reduce_fusion.2
  301.6 2.2 fusion.32
  303.8 0.9 copy-done.1
  304.7 1.7 bitcast_reduce_fusion.2
  307.7 2.2 fusion.32
  309.9 0.9 copy-done.1
  310.8 1.7 bitcast_reduce_fusion.2
  313.8 2.2 fusion.32
  316.0 0.9 copy-done.1
  316.8 1.7 bitcast_reduce_fusion.2
  319.9 2.2 fusion.32
  322.0 0.9 copy-done.1
  322.9 1.6 multiply_reduce_fusion
  324.6 0.7 sqrt_multiply_fusion
  325.3 1.4 fusion.19
  327.4 12.8 %all_to_all.63 = bf16[4,64,768]{2,1,0:T(8,128)(2,1)S(1)} all-to-all(bf16[4,64,768]{2,1,0:T(8,128)(2,1)S(1)} %all_to_all.53), channel_id=1, replica_groups=mesh['patch'=128,'head'=4] {'head'}, dimensions={0} | all-to-all | bytes 786432 | tf_op jit(solution)/shard_map/all_to_all | solution.py:81
  340.2 0.8 copy.39
  (64 shorter events, 6.8 us)
Async XLA Ops:
  6.5 17.8 %copy-start.4 = (bf16[64,3072]{1,0:T(8,128)(2,1)S(1)}, bf16[64,3072]{1,0:T(8,128)(2,1)}, u32[]{:S(2)}) copy-start(bf16[64,3072]{1,0:T(8,128)(2,1)} %param.7) | copy-start | bytes 1179652
  6.5 147.1 %all-gather.3.cloned.1.call-start = ((), (), s32[]{:S(2)}) async-start(), calls=%async_computation.4 | async-start | bytes 3170304 | tf_op jit(solution)/shard_map/all_gather | solution.py:72
  7.6 27.4 %copy-start.5 = (bf16[64,3072]{1,0:T(8,128)(2,1)S(1)}, bf16[64,3072]{1,0:T(8,128)(2,1)}, u32[]{:S(2)}) copy-start(bf16[64,3072]{1,0:T(8,128)(2,1)} %param.5) | copy-start | bytes 1179652
  24.3 262.1 %all-gather.5.cloned.1.call-start = ((), (), s32[]{:S(2)}) async-start(), calls=%async_computation.5 | async-start | bytes 3170304 | tf_op jit(solution)/shard_map/all_gather | solution.py:73
  35.8 11.2 %all-to-all-start.1 = ((bf16[64,4,768]{2,0,1:T(8,128)(2,1)}), bf16[64,4,768]{2,0,1:T(8,128)(2,1)S(1)}, u32[]{:S(2)}, u32[]{:S(2)}) async-start(bf16[64,4,768]{2,0,1:T(8,128)(2,1)} %bitcast.43), calls=%async_computation.1 | async-start | bytes 786432 | tf_op jit(solution)/shard_map/all_to_all | solution.py:58
  300.3 0.7 copy-start.2
  300.3 1.3 copy-start
  301.0 0.6 copy-start.3
  303.8 0.9 copy-start.1
  306.4 0.7 copy-start.2
  306.4 1.3 copy-start
  307.1 0.6 copy-start.3
  309.9 0.9 copy-start.1
  312.5 0.7 copy-start.2
  312.5 1.3 copy-start
  313.2 0.6 copy-start.3
  315.9 0.9 copy-start.1
  318.5 0.7 copy-start.2
  318.6 1.3 copy-start
  319.3 0.6 copy-start.3
  322.0 0.9 copy-start.1
Sparse Core Ops, SparseCore 0:
  24.4 129.2 all-gather.2
  158.0 128.3 all-gather.4
where the time goes:
time: 349 us; the launch traced here: 348 us
  waiting for transfers between devices  233 us (67%)
  blocking collectives  38.5 us (11%)
  local copies, waits for them, and re-layouts  34.8 us (10%)
  matrix products  15.4 us (4%)
  between operations  13.5 us (4%)
  other arithmetic  7.5 us (2%)
  starting transfers between devices  4.51 us (1%)
    all_gather x1, waiting for transfers between devices, shards(): lax.all_gather(value_rows, 'patch', axis=0, tiled=True)  120 us
    all_gather x1, waiting for transfers between devices, shards(): lax.all_gather(key_rows, 'patch', axis=0, tiled=True)  106 us
    all_to_all x1, blocking collectives, shards(): lax.all_to_all(keys, 'head', split_axis=1, concat_axis=0, tiled=True)  15.8 us
    all_to_all x1, blocking collectives, shards(): lax.all_to_all(outgoing, 'head', split_axis=0, concat_axis=1, tiled=True)  12.8 us
    all_to_all x1, blocking collectives, shards(): lax.all_to_all(values, 'head', split_axis=1, concat_axis=0, tiled=True)  9.84 us
    unnamed x7, local copies, waits for them, and re-layouts  9.21 us
    dot_general x4, matrix products, update(): jnp.einsum('hqk,khd->hqd', weights, value_block, preferred_element_type=j...  8.61 us
    reshape x1, local copies, waits for them, and re-layouts, fold_blocks(): key_blocks = key_piece.reshape(total_rows // length, length, heads_here, HD)  7.67 us
  transfers between devices with their start and end apart: 3, of which 3 were waited for; matrix products, arithmetic and copies ran while one was open for 4% of the time, Pallas kernels for 0%

commit v1 on v0

v1 whole, which is shorter than its diff:
```python
import functools

import jax
import jax.numpy as jnp
from jax import lax
from jax.experimental import pallas as pl
from jax.experimental.pallas import tpu as pltpu
from jax.sharding import PartitionSpec as P

HD = 128
POOL = 16
EPS = 1e-6
X, Y, Z, C = 4, 8, 8, 2
MESH = pl.DeviceIdType.MESH
ORDER = (4, 3, 5, 2, 6, 1, 7, 0)
SLOT = {dz: slot for slot, dz in enumerate(ORDER)}


def ring_steps(n):
    full = [(s, t) for s in range(n // 2 - 1) for t in range(2)]
    return full + [(n // 2 - 1, 0)]


def kernel(
    q_hbm, k_hbm, v_hbm, o_hbm,
    kv_in, send_kv, recv_kv, buf1, buf2, qbuf, obuf,
    local_sem, zk_s, zk_r, zq_s, zq_r,
    x1_s, x1_r, yr_s, yr_r, yl_s, yl_r, c1_s, c1_r,
    y2_s, y2_r, xr_s, xr_r, xl_s, xl_r, c2_s, c2_r,
    o_s, o_r,
):
    tokens, width = q_hbm.shape
    cols = width // Z
    heads = cols // HD
    groups = tokens // POOL
    xh = X // 2
    patch, head = lax.axis_index("patch"), lax.axis_index("head")
    y = lax.rem(patch, Y)
    x_hi = lax.rem(lax.div(patch, Y), xh)
    z = lax.div(patch, Y * xh)
    x = x_hi * 2 + lax.div(head, C)
    c = lax.rem(head, C)

    def at(xx, yy, zz, cc):
        return ((zz * xh + lax.div(xx, 2)) * Y + yy, lax.rem(xx, 2) * C + cc)

    def plus(a, d, n):
        return lax.rem(a + d + n, n)

    def z_at(dz):
        return at(x, y, plus(z, dz, Z), c)

    def x_at(dx):
        return at(plus(x, dx, X), y, z, c)

    def y_at(dy):
        return at(x, plus(y, dy, Y), z, c)

    sibling = at(x, y, z, C - 1 - c)

    def remote(src, dst, send, recv, device):
        return pltpu.make_async_remote_copy(
            src_ref=src, dst_ref=dst, send_sem=send, recv_sem=recv,
            device_id=device, device_id_type=MESH,
        )

    barrier = pltpu.get_barrier_semaphore()
    peers = [z_at(d) for d in range(1, Z)] + [x_at(d) for d in range(1, X)]
    peers += [y_at(d) for d in range(1, Y)] + ([sibling] if C > 1 else [])
    for peer in peers:
        pl.semaphore_signal(barrier, inc=1, device_id=peer, device_id_type=MESH)

    load_k = pltpu.make_async_copy(k_hbm, kv_in.at[pl.ds(0, tokens)], local_sem.at[0])
    load_v = pltpu.make_async_copy(v_hbm, kv_in.at[pl.ds(tokens, tokens)], local_sem.at[1])
    own_q = pltpu.make_async_copy(
        q_hbm.at[:, pl.ds(pl.multiple_of(z * cols, HD), cols)], qbuf.at[SLOT[0]], local_sem.at[2]
    )
    load_k.start()
    load_v.start()
    own_q.start()

    row = lax.broadcasted_iota(jnp.int32, (2 * groups, 2 * tokens), 0)
    col = lax.broadcasted_iota(jnp.int32, (2 * groups, 2 * tokens), 1)
    mean = jnp.where(lax.div(col, POOL) == row, 1.0 / POOL, 0.0).astype(jnp.bfloat16)
    load_k.wait()
    load_v.wait()
    pooled = jnp.dot(mean, kv_in[...], preferred_element_type=jnp.float32)
    pad = jnp.zeros((32 - heads * 2 * groups, HD), jnp.float32)
    for zz in range(Z):
        pieces = [pooled[:, (zz * heads + j) * HD : (zz * heads + j + 1) * HD] for j in range(heads)]
        send_kv[zz] = jnp.concatenate(pieces + [pad], axis=0).astype(jnp.bfloat16)
    recv_kv[z] = send_kv[z]

    pl.semaphore_wait(barrier, len(peers))

    waits = []
    kv_copies, q_copies = [], []
    for dz in ORDER[:-1]:
        copy = remote(
            send_kv.at[plus(z, dz, Z)], recv_kv.at[z], zk_s.at[dz - 1], zk_r.at[dz - 1], z_at(dz)
        )
        copy.start()
        waits.append(copy.wait_send)
    for dz in ORDER[:-1]:
        columns = pl.ds(pl.multiple_of(plus(z, dz, Z) * cols, HD), cols)
        copy = remote(
            q_hbm.at[:, columns], qbuf.at[SLOT[dz]], zq_s.at[dz - 1], zq_r.at[dz - 1], z_at(dz)
        )
        copy.start()
        waits.append(copy.wait_send)
        q_copies.append(copy)
    for dz in ORDER[:-1]:
        remote(
            send_kv.at[0], recv_kv.at[plus(z, -dz, Z)], zk_s.at[dz - 1], zk_r.at[dz - 1], z_at(dz)
        ).wait_recv()

    rows = 2 * heads * Z * groups
    row = lax.broadcasted_iota(jnp.int32, (rows, Z * 32), 0)
    col = lax.broadcasted_iota(jnp.int32, (rows, Z * 32), 1)
    which, place = lax.div(row, Z * groups), lax.rem(row, Z * groups)
    wanted = (
        lax.div(place, groups) * 32
        + lax.rem(which, heads) * (2 * groups)
        + lax.div(which, heads) * groups
        + lax.rem(place, groups)
    )
    pick = jnp.where(col == wanted, 1.0, 0.0).astype(jnp.bfloat16)
    block = jnp.dot(pick, recv_kv[...].reshape(Z * 32, HD), preferred_element_type=jnp.float32)
    block = block.astype(jnp.bfloat16).reshape(2 * heads, 2, 16, HD)
    buf1[y, c, x] = block[:, 0]
    buf2[x, c, y] = block[:, 1]

    for dx in range(1, X):
        ref = buf1.at[y, c, x]
        copy = remote(ref, ref, x1_s.at[dx - 1], x1_r.at[dx - 1], x_at(dx))
        copy.start()
        waits.append(copy.wait_send)
    for dy in (4, 3, 5, 2, 6, 1, 7) if Y == 8 else range(1, Y):
        ref = buf2.at[x, c, y]
        copy = remote(ref, ref, y2_s.at[dy - 1], y2_r.at[dy - 1], y_at(dy))
        copy.start()
        waits.append(copy.wait_send)

    half1, half2 = X // 2, Y // 2

    def piece1(i, t, core):
        return buf1.at[plus(y, i, Y), core, pl.ds(t * half1, half1)]

    def piece2(i, t, core):
        return buf2.at[plus(x, i, X), core, pl.ds(t * half2, half2)]

    def ring(n, piece, where, sr, rr, sl, rl, cs, cr):
        right = ring_steps(n)
        arrivals = []

        def share(i, t, number):
            if C > 1:
                copy = remote(piece(i, t, c), piece(i, t, c), cs.at[number], cr.at[number], sibling)
                copy.start()
                waits.append(copy.wait_send)
                other = remote(
                    piece(i, t, 1 - c), piece(i, t, 1 - c), cs.at[number], cr.at[number], sibling
                )
                arrivals.append(other.wait_recv)

        def send(step, t, way):
            i = -step * way
            ref = piece(i, t, c)
            s, r = (sr, rr) if way == 1 else (sl, rl)
            copy = remote(ref, ref, s.at[2 * step + (t if way == 1 else 1 - t)],
                          r.at[2 * step + (t if way == 1 else 1 - t)], where(way))
            copy.start()
            waits.append(copy.wait_send)

        def begin():
            for k in range(2):
                for way in (1, -1):
                    t = k if way == 1 else 1 - k
                    if (0, k) in right:
                        send(0, t, way)
            for t in range(2):
                share(0, t, t)

        def step(number):
            s, k = right[number]
            for way in (1, -1):
                t = k if way == 1 else 1 - k
                i = -(s + 1) * way
                ref = piece(i, t, c)
                ss, rr_ = (sr, rr) if way == 1 else (sl, rl)
                remote(ref, ref, ss.at[2 * s + k], rr_.at[2 * s + k], where(way)).wait_recv()
                if (s + 1, k) in right:
                    send(s + 1, t, way)
                share(i, t, 2 + 2 * number + (0 if way == 1 else 1))

        return begin, [functools.partial(step, number) for number in range(len(right))], arrivals

    begin1, steps1, arrivals1 = ring(Y, piece1, y_at, yr_s, yr_r, yl_s, yl_r, c1_s, c1_r)
    begin2, steps2, arrivals2 = ring(X, piece2, x_at, xr_s, xr_r, xl_s, xl_r, c2_s, c2_r)

    for dx in range(1, X):
        ref = buf1.at[y, c, plus(x, -dx, X)]
        remote(ref, ref, x1_s.at[dx - 1], x1_r.at[dx - 1], x_at(dx)).wait_recv()
    begin1()
    for dy in range(1, Y):
        ref = buf2.at[x, c, plus(y, -dy, Y)]
        remote(ref, ref, y2_s.at[dy - 1], y2_r.at[dy - 1], y_at(dy)).wait_recv()
    begin2()
    todo1, todo2 = list(steps1), list(steps2)
    while todo1 or todo2:
        for _ in range(2):
            if todo1:
                todo1.pop(0)()
        if todo2:
            todo2.pop(0)()

    own_q.wait()
    for copy in q_copies:
        copy.wait_recv()
    for wait in arrivals1 + arrivals2:
        wait()

    scale = HD ** (-0.5)
    part = Z // 2
    rows1, rows2 = Y * C * X * 16, X * C * Y * 16

    def output(slot, j):
        dz = ORDER[slot]
        column = pl.ds(pl.multiple_of(j * HD, HD), HD)
        away = pl.ds(pl.multiple_of(z * cols + j * HD, HD), HD)
        src, dst = obuf.at[slot, :, column], o_hbm.at[:, away]
        number = slot * heads + j
        if dz == 0:
            return pltpu.make_async_copy(src, dst, o_s.at[number])
        return remote(src, dst, o_s.at[number], o_r.at[number], z_at(-dz))

    for half in range(2):
        slots = range(half * part, (half + 1) * part)

        def one_head(j, carry):
            column = pl.ds(pl.multiple_of(j * HD, HD), HD)
            query = qbuf[half * part : (half + 1) * part, :, column].reshape(part * tokens, HD)
            across = (((1,), (1,)), ((), ()))
            key1 = buf1[:, :, :, j].reshape(rows1, HD)
            key2 = buf2[:, :, :, j].reshape(rows2, HD)
            scores1 = lax.dot_general(query, key1, across, preferred_element_type=jnp.float32)
            scores2 = lax.dot_general(query, key2, across, preferred_element_type=jnp.float32)
            peak = jnp.maximum(
                jnp.max(scores1, axis=1, keepdims=True), jnp.max(scores2, axis=1, keepdims=True)
            )
            weights1 = jnp.exp((scores1 - peak) * scale).astype(jnp.bfloat16)
            weights2 = jnp.exp((scores2 - peak) * scale).astype(jnp.bfloat16)
            value1 = buf1[:, :, :, heads + j].reshape(rows1, HD)
            value2 = buf2[:, :, :, heads + j].reshape(rows2, HD)
            value1 = jnp.concatenate([value1, jnp.ones_like(value1)], axis=1)
            value2 = jnp.concatenate([value2, jnp.ones_like(value2)], axis=1)
            both = jnp.dot(weights1, value1, preferred_element_type=jnp.float32)
            both += jnp.dot(weights2, value2, preferred_element_type=jnp.float32)
            mixed = both[:, :HD] / both[:, HD:]
            power = jnp.mean(mixed * mixed, axis=1, keepdims=True)
            normed = (mixed * lax.rsqrt(power + EPS)).astype(jnp.bfloat16)
            obuf[half * part : (half + 1) * part, :, column] = normed.reshape(part, tokens, HD)
            for slot in slots:
                output(slot, j).start()
            return carry

        lax.fori_loop(0, heads, one_head, 0)

    for slot in range(Z):
        for j in range(heads):
            copy = output(slot, j)
            if ORDER[slot] == 0:
                copy.wait()
            else:
                copy.wait_send()
    for slot in range(Z):
        dz = ORDER[slot]
        if dz:
            for j in range(heads):
                away = pl.ds(pl.multiple_of(plus(z, dz, Z) * cols + j * HD, HD), HD)
                number = slot * heads + j
                remote(
                    obuf.at[slot, :, pl.ds(j * HD, HD)], o_hbm.at[:, away],
                    o_s.at[number], o_r.at[number], z_at(-dz),
                ).wait_recv()
    for wait in waits:
        wait()


def shards(queries, keys, values):
    tokens, width = queries.shape
    cols = width // Z
    heads = cols // HD
    dma = pltpu.SemaphoreType.DMA
    bf16 = jnp.bfloat16
    n1, n2 = 2 * Y, 2 * X
    sems = [3, Z - 1, Z - 1, Z - 1, Z - 1]
    sems += [X - 1, X - 1] + [Y] * 4 + [n1, n1]
    sems += [Y - 1, Y - 1] + [X] * 4 + [n2, n2]
    sems += [Z * heads, Z * heads]
    return pl.pallas_call(
        kernel,
        out_shape=jax.ShapeDtypeStruct(queries.shape, bf16),
        in_specs=[pl.BlockSpec(memory_space=pl.ANY)] * 3,
        out_specs=pl.BlockSpec(memory_space=pl.ANY),
        scratch_shapes=[
            pltpu.VMEM((2 * tokens, width), bf16),
            pltpu.VMEM((Z, 32, HD), bf16),
            pltpu.VMEM((Z, 32, HD), bf16),
            pltpu.VMEM((Y, C, X, 2 * heads, 16, HD), bf16),
            pltpu.VMEM((X, C, Y, 2 * heads, 16, HD), bf16),
            pltpu.VMEM((Z, tokens, cols), bf16),
            pltpu.VMEM((Z, tokens, cols), bf16),
        ]
        + [dma((max(n, 1),)) for n in sems],
        compiler_params=pltpu.CompilerParams(
            collective_id=0, has_side_effects=True, vmem_limit_bytes=48 * 2**20
        ),
    )(queries, keys, values)


def solution(mesh):
    spec = P(("patch", "head"), None)
    return jax.shard_map(
        shards, mesh=mesh, in_specs=(spec, spec, spec), out_specs=spec, check_vma=False
    )
```

time: 349 us -> 58.2 us (0.17)
  waiting for transfers between devices: 233 us -> 0 us
  Pallas kernels: 0 us -> 54.2 us
  blocking collectives: 38.5 us -> 0 us
  local copies, waits for them, and re-layouts: 34.8 us -> 3.73 us
  matrix products: 15.4 us -> 0 us
  between operations: 13.5 us -> 0.01 us
  other arithmetic: 7.5 us -> 0 us
  starting transfers between devices: 4.51 us -> 0 us
    all_gather x2 -> x0, waiting for transfers between devices: 227 us -> none  [the longest x1 120 us: shards(): lax.all_gather(value_rows, 'patch', axis=0, tiled=True)]
    pallas_call x0 -> x1, Pallas kernels: none -> 54.2 us  [shards(): pl.pallas_call(kernel, out_shape=jax.ShapeDtypeStruct(queries.shape, bf16...]
    all_to_all x3 -> x0, blocking collectives: 38.5 us -> none  [the longest x1 15.8 us: shards(): lax.all_to_all(keys, 'head', split_axis=1, concat_axis=0, tiled=True)]
    reshape x3 -> x0, local copies, waits for them, and re-layouts: 15.8 us -> none  [the longest x1 7.67 us: fold_blocks(): key_blocks = key_piece.reshape(total_rows // length, length, heads_here, HD)]
    dot_general x8 -> x0, matrix products: 15.4 us -> none  [the longest x4 8.61 us: update(): jnp.einsum('hqk,khd->hqd', weights, value_block, preferred_element_type=j...]
    all_to_all x1 -> x0, waiting for transfers between devices: 6.75 us -> none  [shards(): lax.all_to_all(queries, 'head', split_axis=1, concat_axis=0, tiled=True)]
    while x36 -> x0, local copies, waits for them, and re-layouts: 6.44 us -> none
    unnamed x7, local copies, waits for them, and re-layouts: 9.21 us -> 3.73 us
  transfers between devices with their start and end apart: 3 -> 0, of which waited for: 3 -> 0; matrix products, arithmetic and copies ran while one was open for 4% -> 0% of each run, Pallas kernels for 0% -> 0%
where the time goes in v1:
time: 58.2 us; the launch traced here: 58 us
  Pallas kernels  54.2 us (93%)
  local copies, waits for them, and re-layouts  3.73 us (6%)
    pallas_call x1, Pallas kernels, shards(): pl.pallas_call(kernel, out_shape=jax.ShapeDtypeStruct(queries.shape, bf16...  54.2 us
    unnamed x7, local copies, waits for them, and re-layouts  3.73 us

profile of v1, /device:TPU:1, one launch (start us, length us, event | category | flops | bytes accessed | tf_op | source)
XLA Modules:
  0.0 58.0 jit_solution(13444931113294116971)
XLA Ops:
  0.0 0.0 copy-start
  0.0 1.0 %copy-done = bf16[64,3072]{1,0:T(8,128)(2,1)S(1)} copy-done((bf16[64,3072]{1,0:T(8,128)(2,1)S(1)}, bf16[64,3072]{1,0:T(8,128)(2,1)}, u32[]{:S(2)}) %copy-start) | copy-done | bytes 393240
  1.0 0.0 copy-start.1
  1.0 1.0 %copy-done.1 = bf16[64,3072]{1,0:T(8,128)(2,1)S(1)} copy-done((bf16[64,3072]{1,0:T(8,128)(2,1)S(1)}, bf16[64,3072]{1,0:T(8,128)(2,1)}, u32[]{:S(2)}) %copy-start.1) | copy-done | bytes 393240
  2.0 0.0 copy-start.2
  2.0 1.0 %copy-done.2 = bf16[64,3072]{1,0:T(8,128)(2,1)S(1)} copy-done((bf16[64,3072]{1,0:T(8,128)(2,1)S(1)}, bf16[64,3072]{1,0:T(8,128)(2,1)}, u32[]{:S(2)}) %copy-start.2) | copy-done | bytes 393240
  3.0 54.2 %shard_map.37 = bf16[64,3072]{1,0:T(8,128)(2,1)S(1)} custom-call(bf16[64,3072]{1,0:T(8,128)(2,1)S(1)} %copy-done, bf16[64,3072]{1,0:T(8,128)(2,1)S(1)} %copy-done.1, bf16[64,3072]{1,0:T(8,128)(2,1)S(1)} %copy-done.2), custom_call_target="tpu_custom_call" | custom-call | tf_op jit(solution)/shard_map/pallas_call | solution.py:301
  57.2 0.7 %copy.5 = bf16[64,3072]{1,0:T(8,128)(2,1)} copy(bf16[64,3072]{1,0:T(8,128)(2,1)S(1)} %shard_map.37) | data formatting | bytes 786432
Async XLA Ops:
  0.0 1.0 %copy-start = (bf16[64,3072]{1,0:T(8,128)(2,1)S(1)}, bf16[64,3072]{1,0:T(8,128)(2,1)}, u32[]{:S(2)}) copy-start(bf16[64,3072]{1,0:T(8,128)(2,1)} %q_hbm.1) | copy-start | bytes 1179652
  1.0 1.0 %copy-start.1 = (bf16[64,3072]{1,0:T(8,128)(2,1)S(1)}, bf16[64,3072]{1,0:T(8,128)(2,1)}, u32[]{:S(2)}) copy-start(bf16[64,3072]{1,0:T(8,128)(2,1)} %k_hbm.1) | copy-start | bytes 1179652
  2.0 1.0 %copy-start.2 = (bf16[64,3072]{1,0:T(8,128)(2,1)S(1)}, bf16[64,3072]{1,0:T(8,128)(2,1)}, u32[]{:S(2)}) copy-start(bf16[64,3072]{1,0:T(8,128)(2,1)} %v_hbm.1) | copy-start | bytes 1179652

commit v2 on v0

v2 whole, which is shorter than its diff:
```python
import functools

import jax
import jax.numpy as jnp
from jax import lax
from jax.experimental import pallas as pl
from jax.experimental.pallas import tpu as pltpu
from jax.sharding import PartitionSpec as P

HD = 128
POOL = 16
EPS = 1e-6
VMEM_BYTES = (64 * 1024 - 10880) * 2**10
X, Y, Z, C = 4, 8, 8, 2
MESH = pl.DeviceIdType.MESH
ORDER = (4, 3, 5, 2, 6, 1, 7, 0)
SLOT = {dz: slot for slot, dz in enumerate(ORDER)}


FIRST = 5
GROUPS = (4, 3)
THROTTLE1 = True
PLAN = ("b", "s", "t0", "n", "t1", "f", "g0", "e", "g1", "c")
HEADS_FIRST = True
CHUNK = 512


def kernel(
    q_hbm, k_hbm, v_hbm, o_hbm,
    kv_in, send_kv, recv_kv, kv_buf, qbuf, obuf,
    local_sem, zk_s, zk_r, zq_s, zq_r, y2_s, y2_r, x2_s, x2_r, c2_s, c2_r,
    x1_s, x1_r, y1_s, y1_r, c1_s, c1_r, o_s, o_r,
):
    tokens, width = q_hbm.shape
    cols = width // Z
    heads = cols // HD
    groups = tokens // POOL
    xh = X // 2
    patch, head = lax.axis_index("patch"), lax.axis_index("head")
    y = lax.rem(patch, Y)
    x_hi = lax.rem(lax.div(patch, Y), xh)
    z = lax.div(patch, Y * xh)
    x = x_hi * 2 + lax.div(head, C)
    c = lax.rem(head, C)

    def at(xx, yy, zz, cc):
        return ((zz * xh + lax.div(xx, 2)) * Y + yy, lax.rem(xx, 2) * C + cc)

    def plus(a, d, n):
        return lax.rem(a + d + n, n)

    def z_at(dz):
        return at(x, y, plus(z, dz, Z), c)

    def x_at(dx):
        return at(plus(x, dx, X), y, z, c)

    def y_at(dy):
        return at(x, plus(y, dy, Y), z, c)

    sibling = at(x, y, z, C - 1 - c)

    def remote(src, dst, send, recv, device):
        return pltpu.make_async_remote_copy(
            src_ref=src, dst_ref=dst, send_sem=send, recv_sem=recv,
            device_id=device, device_id_type=MESH,
        )

    barrier = pltpu.get_barrier_semaphore()
    peers = [z_at(d) for d in range(1, Z)] + [x_at(d) for d in range(1, X)]
    peers += [y_at(d) for d in range(1, Y)] + ([sibling] if C > 1 else [])
    load_k = pltpu.make_async_copy(k_hbm, kv_in.at[pl.ds(0, tokens)], local_sem.at[0])
    load_v = pltpu.make_async_copy(v_hbm, kv_in.at[pl.ds(tokens, tokens)], local_sem.at[1])
    own_q = pltpu.make_async_copy(
        q_hbm.at[:, pl.ds(pl.multiple_of(z * cols, HD), cols)], qbuf.at[SLOT[0]], local_sem.at[2]
    )
    load_k.start()
    load_v.start()

    for peer in peers:
        pl.semaphore_signal(barrier, inc=1, device_id=peer, device_id_type=MESH)

    own_q.start()

    row = lax.broadcasted_iota(jnp.int32, (2 * groups, 2 * tokens), 0)
    col = lax.broadcasted_iota(jnp.int32, (2 * groups, 2 * tokens), 1)
    mean = jnp.where(lax.div(col, POOL) == row, 1.0 / POOL, 0.0).astype(jnp.bfloat16)
    load_k.wait()
    load_v.wait()
    pooled = jnp.dot(mean, kv_in[...], preferred_element_type=jnp.float32)
    pad = jnp.zeros((32 - heads * 2 * groups, HD), jnp.float32)
    for zz in range(Z):
        pieces = [pooled[:, (zz * heads + j) * HD : (zz * heads + j + 1) * HD] for j in range(heads)]
        send_kv[zz] = jnp.concatenate(pieces + [pad], axis=0).astype(jnp.bfloat16)
    recv_kv[z] = send_kv[z]

    pl.semaphore_wait(barrier, len(peers))

    def wait(ref, sem):
        pltpu.make_async_copy(ref, ref, sem).wait()

    for dz in ORDER[:-1]:
        remote(send_kv.at[plus(z, dz, Z)], recv_kv.at[z], zk_s, zk_r, z_at(dz)).start()
    for dz in ORDER[:-1]:
        columns = pl.ds(pl.multiple_of(plus(z, dz, Z) * cols, HD), cols)
        remote(q_hbm.at[:, columns], qbuf.at[SLOT[dz]], zq_s, zq_r, z_at(dz)).start()
    wait(recv_kv.at[pl.ds(0, Z - 1)], zk_r)

    pieces = 4 * heads
    row = lax.broadcasted_iota(jnp.int32, (pieces * 16, Z * 32), 0)
    col = lax.broadcasted_iota(jnp.int32, (pieces * 16, Z * 32), 1)
    piece = lax.div(row, 16)
    place = lax.rem(lax.div(piece, heads), 2) * 16 + lax.rem(row, 16)
    wanted = (
        lax.div(place, groups) * 32
        + lax.rem(piece, heads) * (2 * groups)
        + lax.div(piece, 2 * heads) * groups
        + lax.rem(place, groups)
    )
    pick = jnp.where(col == wanted, 1.0, 0.0).astype(jnp.bfloat16)
    block = jnp.dot(pick, recv_kv[...].reshape(Z * 32, HD), preferred_element_type=jnp.float32)
    kv_buf[:, x, c, y] = block.astype(jnp.bfloat16).reshape(pieces, 16, HD)

    def go(ref, send, recv, device):
        remote(ref, ref, send, recv, device).start()

    first = pl.ds(0, FIRST)
    second = [pl.ds(FIRST + sum(GROUPS[:k]), GROUPS[k]) for k in range(len(GROUPS))]
    far_y = (4, 3, 5, 2, 6, 1, 7) if Y == 8 else tuple(range(1, Y))
    far_x = (2, 1, 3) if X == 4 else tuple(range(1, X))
    low, high = pl.ds(0, X // 2), pl.ds(X // 2, X // 2)

    def column(dy, some=slice(None)):
        return kv_buf.at[first, some, c, plus(y, dy, Y)]

    def line(k, dx):
        return kv_buf.at[second[k], plus(x, dx, X), c]

    def columns1(n):
        return kv_buf.at[first, :, 0, pl.ds(0, n)]

    def lines2(k, n):
        return kv_buf.at[second[k], pl.ds(0, n), 0]

    def share(ref, send, recv):
        if C > 1:
            go(ref, send, recv, sibling)

    def pushes2(k):
        return kv_buf.at[second[k], 0, 0, pl.ds(0, Y - 1)]

    def begin():
        for dx in far_x:
            go(kv_buf.at[first, x, c, y], x1_s, x1_r, x_at(dx))
        for k in range(len(GROUPS)):
            if k:
                wait(pushes2(k - 1), y2_s.at[k - 1])
            for dy in far_y:
                go(kv_buf.at[second[k], x, c, y], y2_s.at[k], y2_r.at[k], y_at(dy))

    def spread1():
        wait(kv_buf.at[first, pl.ds(0, X - 1), 0, 0], x1_r)
        for dy in (2, -2):
            go(column(0), y1_s.at[0], y1_r.at[0], y_at(dy))
        if not THROTTLE1:
            near1()
        share(column(0), c1_s, c1_r)

    def near1():
        if THROTTLE1:
            wait(columns1(2), y1_s.at[0])
        for dy in (1, -1):
            go(column(0), y1_s.at[1], y1_r.at[1], y_at(dy))

    def spread2(k):
        wait(pushes2(k), y2_r.at[k])
        for dx in far_x:
            go(line(k, 0), x2_s.at[k], x2_r.at[k, 1 if 2 * dx == X else 0], x_at(dx))
        share(line(k, 0), c2_s.at[k], c2_r.at[k])

    def forward1():
        wait(columns1(2), y1_r.at[0])
        for way, some in ((1, low), (-1, high)):
            go(column(-2 * way), y1_s.at[1], y1_r.at[2], y_at(way))
            go(column(-2 * way, some), y1_s.at[1], y1_r.at[3], y_at(2 * way))
        for dy in (2, -2):
            share(column(dy), c1_s, c1_r)
        wait(columns1(2), y1_r.at[1])
        for dy in (1, -1):
            share(column(dy), c1_s, c1_r)

    def finish1():
        wait(columns1(2), y1_r.at[2])
        for dy in (3, -3):
            share(column(dy), c1_s, c1_r)
        wait(columns1(1), y1_r.at[3])
        share(column(4), c1_s, c1_r)

    def finish2(k):
        near = [dx for dx in far_x if 2 * dx != X]
        if near:
            wait(lines2(k, len(near)), x2_r.at[k, 0])
        for dx in near:
            share(line(k, -dx), c2_s.at[k], c2_r.at[k])
        wait(lines2(k, 1), x2_r.at[k, 1])
        share(line(k, -X // 2), c2_s.at[k], c2_r.at[k])

    def complete():
        if C > 1:
            for k in range(len(GROUPS)):
                wait(lines2(k, X), c2_r.at[k])
            wait(columns1(Y), c1_r)

    scale = HD ** (-0.5)
    part = Z // 2
    keys_all = 2 * X * C * Y * 16

    def output(slot, j):
        dz = ORDER[slot]
        column = pl.ds(pl.multiple_of(j * HD, HD), HD)
        away = pl.ds(pl.multiple_of(z * cols + j * HD, HD), HD)
        src, dst = obuf.at[slot, :, column], o_hbm.at[:, away]
        if dz == 0:
            return pltpu.make_async_copy(src, dst, local_sem.at[3])
        return remote(src, dst, o_s, o_r, z_at(-dz))

    def attend(j, half):
        here = slice(half * part, (half + 1) * part)
        column = slice(j * HD, (j + 1) * HD)
        query = qbuf[here, :, column].reshape(part * tokens, HD)
        keys = [kv_buf[k * heads + j].reshape(keys_all // 2, HD) for k in (0, 1)]
        values = [kv_buf[k * heads + j].reshape(keys_all // 2, HD) for k in (2, 3)]
        values = [jnp.concatenate([v, jnp.ones_like(v)], axis=1) for v in values]
        across = (((1,), (1,)), ((), ()))
        peak, both = None, None
        for k in range(0, keys_all, CHUNK):
            part_of, at_row = divmod(k, keys_all // 2)
            rows = slice(at_row, at_row + CHUNK)
            scores = lax.dot_general(
                query, keys[part_of][rows], across, preferred_element_type=jnp.float32
            )
            new = jnp.max(scores, axis=1, keepdims=True)
            if k:
                new = jnp.maximum(peak, new)
            weights = jnp.exp((scores - new) * scale).astype(jnp.bfloat16)
            term = jnp.dot(weights, values[part_of][rows], preferred_element_type=jnp.float32)
            both = both * jnp.exp((peak - new) * scale) + term if k else term
            peak = new
        mixed = both[:, :HD] / both[:, HD:]
        power = jnp.mean(mixed * mixed, axis=1, keepdims=True)
        normed = (mixed * lax.rsqrt(power + EPS)).astype(jnp.bfloat16)
        obuf[here, :, column] = normed.reshape(part, tokens, HD)
        for slot in range(Z)[here]:
            output(slot, j).start()

    def queries_here():
        own_q.wait()
        wait(qbuf.at[pl.ds(0, Z - 1)], zq_r)

    steps = {
        "b": begin, "s": spread1, "t": spread2, "f": forward1, "e": finish1, "g": finish2, "n": near1,
        "c": complete,
    }
    for word in PLAN:
        if word != "n" or THROTTLE1:
            steps[word[0]](*(int(digit) for digit in word[1:]))
    queries_here()
    units = [(j, half) for j in range(heads) for half in range(2)]
    for j, half in units if HEADS_FIRST else sorted(units, key=lambda unit: unit[1]):
        attend(j, half)

    mine = obuf.at[SLOT[0]]
    wait(mine, local_sem.at[3])
    wait(obuf.at[pl.ds(0, Z - 1)], o_s)
    wait(obuf.at[pl.ds(0, Z - 1)], o_r)
    wait(send_kv.at[pl.ds(0, Z - 1)], zk_s)
    wait(qbuf.at[pl.ds(0, Z - 1)], zq_s)
    wait(kv_buf.at[first, pl.ds(0, X - 1), 0, 0], x1_s)
    if THROTTLE1:
        wait(columns1(5), y1_s.at[1])
    else:
        wait(columns1(2), y1_s.at[0])
        wait(columns1(5), y1_s.at[1])
    wait(pushes2(len(GROUPS) - 1), y2_s.at[len(GROUPS) - 1])
    for k in range(len(GROUPS)):
        wait(lines2(k, X - 1), x2_s.at[k])
        if C > 1:
            wait(lines2(k, X), c2_s.at[k])
    if C > 1:
        wait(columns1(Y), c1_s)


def shards(queries, keys, values):
    tokens, width = queries.shape
    cols = width // Z
    heads = cols // HD
    dma = pltpu.SemaphoreType.DMA
    bf16 = jnp.bfloat16
    return pl.pallas_call(
        kernel,
        out_shape=jax.ShapeDtypeStruct(queries.shape, bf16),
        in_specs=[pl.BlockSpec(memory_space=pltpu.HBM)] * 3,
        out_specs=pl.BlockSpec(memory_space=pl.ANY),
        scratch_shapes=[
            pltpu.VMEM((2 * tokens, width), bf16),
            pltpu.VMEM((Z, 32, HD), bf16),
            pltpu.VMEM((Z, 32, HD), bf16),
            pltpu.VMEM((4 * heads, X, C, Y, 16, HD), bf16),
            pltpu.VMEM((Z, tokens, cols), bf16),
            pltpu.VMEM((Z, tokens, cols), bf16),
        ]
        + [dma((4,))]
        + [dma] * 4
        + [dma((len(GROUPS),))] * 3
        + [dma((len(GROUPS), 2))]
        + [dma((len(GROUPS),))] * 2
        + [dma] * 2
        + [dma((2,)), dma((4,))]
        + [dma] * 4,
        compiler_params=pltpu.CompilerParams(
            collective_id=0, has_side_effects=True, vmem_limit_bytes=VMEM_BYTES
        ),
    )(queries, keys, values)


def solution(mesh):
    spec = P(("patch", "head"), None)
    return jax.shard_map(
        shards, mesh=mesh, in_specs=(spec, spec, spec), out_specs=spec, check_vma=False
    )
```

time: 349 us -> 50.8 us (0.15)
  waiting for transfers between devices: 233 us -> 0 us
  Pallas kernels: 0 us -> 49.9 us
  blocking collectives: 38.5 us -> 0 us
  local copies, waits for them, and re-layouts: 34.8 us -> 0.75 us
  matrix products: 15.4 us -> 0 us
  between operations: 13.5 us -> 0.01 us
  other arithmetic: 7.5 us -> 0 us
  starting transfers between devices: 4.51 us -> 0 us
    all_gather x2 -> x0, waiting for transfers between devices: 227 us -> none  [the longest x1 120 us: shards(): lax.all_gather(value_rows, 'patch', axis=0, tiled=True)]
    pallas_call x0 -> x1, Pallas kernels: none -> 49.9 us  [shards(): pl.pallas_call(kernel, out_shape=jax.ShapeDtypeStruct(queries.shape, bf16...]
    all_to_all x3 -> x0, blocking collectives: 38.5 us -> none  [the longest x1 15.8 us: shards(): lax.all_to_all(keys, 'head', split_axis=1, concat_axis=0, tiled=True)]
    reshape x3 -> x0, local copies, waits for them, and re-layouts: 15.8 us -> none  [the longest x1 7.67 us: fold_blocks(): key_blocks = key_piece.reshape(total_rows // length, length, heads_here, HD)]
    dot_general x8 -> x0, matrix products: 15.4 us -> none  [the longest x4 8.61 us: update(): jnp.einsum('hqk,khd->hqd', weights, value_block, preferred_element_type=j...]
    unnamed x7 -> x1, local copies, waits for them, and re-layouts: 9.21 us -> 0.75 us
    all_to_all x1 -> x0, waiting for transfers between devices: 6.75 us -> none  [shards(): lax.all_to_all(queries, 'head', split_axis=1, concat_axis=0, tiled=True)]
    while x36 -> x0, local copies, waits for them, and re-layouts: 6.44 us -> none
  transfers between devices with their start and end apart: 3 -> 0, of which waited for: 3 -> 0; matrix products, arithmetic and copies ran while one was open for 4% -> 0% of each run, Pallas kernels for 0% -> 0%
where the time goes in v2:
time: 50.8 us; the launch traced here: 50.7 us
  Pallas kernels  49.9 us (98%)
  local copies, waits for them, and re-layouts  0.75 us (1%)
    pallas_call x1, Pallas kernels, shards(): pl.pallas_call(kernel, out_shape=jax.ShapeDtypeStruct(queries.shape, bf16...  49.9 us

profile of v2, /device:TPU:1, one launch (start us, length us, event | category | flops | bytes accessed | tf_op | source)
XLA Modules:
  0.0 50.7 jit_solution(14775272493709155418)
XLA Ops:
  0.0 49.9 %shard_map.37 = bf16[64,3072]{1,0:T(8,128)(2,1)S(1)} custom-call(bf16[64,3072]{1,0:T(8,128)(2,1)} %q_hbm.1, bf16[64,3072]{1,0:T(8,128)(2,1)} %k_hbm.1, bf16[64,3072]{1,0:T(8,128)(2,1)} %v_hbm.1), custom_call_target="tpu_custom_call" | custom-call | tf_op jit(solution)/shard_map/pallas_call | solution.py:299
  49.9 0.7 %copy.5 = bf16[64,3072]{1,0:T(8,128)(2,1)} copy(bf16[64,3072]{1,0:T(8,128)(2,1)S(1)} %shard_map.37) | data formatting | bytes 786432

commit v3 on v2

--- a/solution.py
+++ b/solution.py
@@ -212,7 +212,7 @@
             wait(columns1(Y), c1_r)
 
     scale = HD ** (-0.5)
-    part = Z // 2
+    part = Z // 4
     keys_all = 2 * X * C * Y * 16
 
     def output(slot, j):
@@ -265,7 +265,7 @@
         if word != "n" or THROTTLE1:
             steps[word[0]](*(int(digit) for digit in word[1:]))
     queries_here()
-    units = [(j, half) for j in range(heads) for half in range(2)]
+    units = [(j, half) for j in range(heads) for half in range(4)]
     for j, half in units if HEADS_FIRST else sorted(units, key=lambda unit: unit[1]):
         attend(j, half)
 

time: 50.8 us -> 51.3 us (level)
    pallas_call x1, Pallas kernels: 49.9 us -> 50.4 us  [shards(): pl.pallas_call(kernel, out_shape=jax.ShapeDtypeStruct(queries.shape, bf16...]
where the time goes in v3:
time: 51.3 us; the launch traced here: 51.2 us
  Pallas kernels  50.4 us (98%)
  local copies, waits for them, and re-layouts  0.75 us (1%)
    pallas_call x1, Pallas kernels, shards(): pl.pallas_call(kernel, out_shape=jax.ShapeDtypeStruct(queries.shape, bf16...  50.4 us

profile of v3, /device:TPU:1, one launch (start us, length us, event | category | flops | bytes accessed | tf_op | source)
XLA Modules:
  0.0 51.2 jit_solution(3149965578839257)
XLA Ops:
  0.0 50.4 %shard_map.37 = bf16[64,3072]{1,0:T(8,128)(2,1)S(1)} custom-call(bf16[64,3072]{1,0:T(8,128)(2,1)} %q_hbm.1, bf16[64,3072]{1,0:T(8,128)(2,1)} %k_hbm.1, bf16[64,3072]{1,0:T(8,128)(2,1)} %v_hbm.1), custom_call_target="tpu_custom_call" | custom-call | tf_op jit(solution)/shard_map/pallas_call | solution.py:299
  50.4 0.7 %copy.5 = bf16[64,3072]{1,0:T(8,128)(2,1)} copy(bf16[64,3072]{1,0:T(8,128)(2,1)S(1)} %shard_map.37) | data formatting | bytes 786432
